TPU v7x, 32 devices: a whole 2x2x4 slice. The times are simulated.
32 devices in a mesh: groups: 2 (over x), seq: 8 (over z, y), tensor: 2 (over core).
Axes of the slice: x: 2, y: 2, z: 4, core: 2. Of those that a mesh axis runs over, the one named last changes fastest.
Arguments:
- queries: bfloat16 [2048, 4096], P(('groups', 'seq'), 'tensor'), parts along dimension 0, may hold values from -80 to 80
- resp_keys: bfloat16 [2048, 512], P(('groups', 'seq'), 'tensor'), parts along dimension 0, may hold values from -18 to 18
- resp_values: bfloat16 [2048, 512], P(('groups', 'seq'), 'tensor'), parts along dimension 0, may hold values from -24 to 24
- prompt_keys: bfloat16 [16384, 512], P(('groups', 'seq'), 'tensor'), parts along dimension 0, may hold values from -12 to 12
- prompt_values: bfloat16 [16384, 512], P(('groups', 'seq'), 'tensor'), parts along dimension 0, may hold values from -24 to 24
- response_prompt: int32 [64, 1], P(('groups', 'seq')), parts along dimension 0, may hold values from 0 to 3; in each aligned block of 4 rows (0 to 3, 4 to 7, ...) no two rows name the same one
- response_lengths: int32 [16, 4], P(('groups', 'seq')), parts along dimension 0, may hold values from 1 to 40, 128 in all within a row
- shard_order: int32 [16], P('groups'), parts along dimension 0, may hold values from 0 to 7, each once
Outputs:
- attended: bfloat16 [2048, 4096], P(('groups', 'seq'), 'tensor'), parts along dimension 0
There are 2 independent parts, one for each index of `groups`. A program takes and returns all parts, laid end to end along the dimension named above; each array names one. Nothing has to cross between parts.
Inputs may be any that keep to these rules, and one draw needn't show every extreme that they name: `response_prompt`: the responses of one pack belong to different prompts. `response_lengths`: the lengths of one pack add up to 128; the longest response of every pack has 40 tokens. `shard_order`: A permutation of 0 .. 7.
All inputs are finite; a program needn't handle non-finite values.
Results may differ from a plain program's by a relative error of at most 0.0056.
Values may be sent and summed in bfloat16 or wider, within the bound.
A program may use at most 64 MiB of HBM per device.

v0:
```python
import math

import jax
import jax.numpy as jnp
from jax import lax
from jax.sharding import PartitionSpec as P

HD = 128
PROMPTS = 4
LEN_MOST = 40


def as_sent(x):

    def short(part):
        return part.astype(jnp.bfloat16) if part.dtype == jnp.float32 else part

    return jax.tree.map(short, x)


def attend(rows, keys, values, key_heads, head_dim, allowed):
    row_count = rows.shape[0]
    head_count = rows.shape[1] // head_dim
    grouping = head_count // key_heads
    scaling = 1.0 / math.sqrt(head_dim)
    results = []
    log_parts = []
    for kv_index in range(key_heads):
        query_rows = rows[:, kv_index * grouping * head_dim : (kv_index + 1) * grouping * head_dim]
        query_rows = query_rows.reshape(row_count * grouping, head_dim)
        key_part = keys[:, kv_index * head_dim : (kv_index + 1) * head_dim]
        value_part = values[:, kv_index * head_dim : (kv_index + 1) * head_dim]
        scores = (
            lax.dot_general(
                query_rows, key_part, (((1,), (1,)), ((), ())), preferred_element_type=jnp.float32
            )
            * scaling
        )
        if allowed is not None:
            scores = jnp.where(jnp.repeat(allowed, grouping, axis=0), scores, -1e30)
        highest = jnp.max(scores, axis=1, keepdims=True)
        summed = jnp.sum(jnp.exp(scores - highest), axis=1, keepdims=True)
        log_total = highest + jnp.log(summed)
        weights = jnp.exp(scores - log_total).astype(jnp.bfloat16)
        result = jnp.dot(weights, value_part, preferred_element_type=jnp.float32)
        results.append(result.reshape(row_count, grouping * head_dim))
        log_parts.append(log_total.reshape(row_count, grouping))
    return (jnp.concatenate(results, axis=1), jnp.concatenate(log_parts, axis=1))


def combine(parts_out, parts_log, head_dim):
    stacked = jnp.stack(parts_log)
    highest = jnp.max(stacked, axis=0)
    total_log = highest + jnp.log(jnp.sum(jnp.exp(stacked - highest), axis=0))
    row_count, head_count = total_log.shape
    blended = jnp.zeros((row_count, head_count, head_dim), jnp.float32)
    for result, log_part in zip(parts_out, parts_log):
        blended = blended + jnp.exp(log_part - total_log)[:, :, None] * result.reshape(
            row_count, head_count, head_dim
        )
    return blended.reshape(row_count, head_count * head_dim).astype(jnp.bfloat16)


def per_device(
    queries,
    resp_keys,
    resp_values,
    prompt_keys,
    prompt_values,
    response_prompt,
    response_lengths,
    shard_order,
):
    devices = lax.axis_size("seq")
    shard_count = devices // PROMPTS
    tok_rows = queries.shape[0]
    key_heads = resp_keys.shape[1] // HD
    capacity = LEN_MOST
    lengths = response_lengths[0]
    prompts = response_prompt[:, 0]
    finish = jnp.cumsum(lengths)
    starts = finish - lengths
    device_ids = jnp.arange(devices, dtype=jnp.int32)
    inverse = jnp.sum(
        jnp.where(shard_order[None, :] == device_ids[:, None], device_ids[None, :], 0), axis=1
    )
    shard_prompt = shard_order // shard_count
    matched = shard_prompt[:, None] == prompts[None, :]
    first_rows = jnp.sum(jnp.where(matched, starts[None, :], 0), axis=1)
    live_rows = jnp.sum(jnp.where(matched, lengths[None, :], 0), axis=1)
    slot_ids = jnp.arange(capacity, dtype=jnp.int32)
    row_ids = jnp.minimum(first_rows[:, None] + slot_ids[None, :], tok_rows - 1)
    is_live = slot_ids[None, :] < live_rows[:, None]
    picked = jnp.take(queries, row_ids.reshape(-1), axis=0).reshape(
        devices, capacity, queries.shape[1]
    )
    outgoing = jnp.where(is_live[:, :, None], picked, 0)
    token_ids = jnp.arange(tok_rows, dtype=jnp.int32)
    segment = jnp.sum((token_ids[:, None] >= starts[None, :]).astype(jnp.int32), axis=1) - 1
    offset = token_ids - jnp.take(starts, segment)
    token_prompt = jnp.take(prompts, segment)
    allowed = (segment[:, None] == segment[None, :]) & (token_ids[None, :] <= token_ids[:, None])
    received = lax.all_to_all(outgoing, "seq", split_axis=0, concat_axis=0, tiled=True)
    dims_in = received.shape
    row_count = dims_in[0] * dims_in[1]
    block_rows = math.gcd(row_count, 64)
    pieces = received.reshape(row_count // block_rows, block_rows, dims_in[2])

    def owner_one_block(piece_rows):
        result, log_part = attend(piece_rows, prompt_keys, prompt_values, key_heads, HD, None)
        return (result.astype(jnp.bfloat16), log_part)

    result, log_part = lax.map(owner_one_block, pieces)
    part_out = result.reshape(dims_in[0], dims_in[1], -1)
    part_log = log_part.reshape(dims_in[0], dims_in[1], -1)
    back_out = lax.all_to_all(
        as_sent(part_out), "seq", split_axis=0, concat_axis=0, tiled=True
    ).astype(part_out.dtype)
    back_log = lax.all_to_all(part_log, "seq", split_axis=0, concat_axis=0, tiled=True)
    block_rows = math.gcd(tok_rows, 64)
    pieces = queries.reshape(tok_rows // block_rows, block_rows, queries.shape[1])
    rules = allowed.reshape(tok_rows // block_rows, block_rows, tok_rows)

    def local_one_block(inputs):
        return attend(inputs[0], resp_keys, resp_values, key_heads, HD, inputs[1])

    result, log_part = lax.map(local_one_block, (pieces, rules))
    local_out = result.reshape(tok_rows, -1)
    local_log = log_part.reshape(tok_rows, -1)
    flat_out = back_out.reshape(devices * capacity, back_out.shape[2])
    flat_log = back_log.reshape(devices * capacity, back_log.shape[2])
    parts_out = [local_out]
    parts_log = [local_log]
    for shard_rank in range(shard_count):
        owner_dev = jnp.take(inverse, token_prompt * shard_count + shard_rank)
        flat_index = owner_dev * capacity + offset
        parts_out.append(jnp.take(flat_out, flat_index, axis=0).astype(jnp.float32))
        parts_log.append(jnp.take(flat_log, flat_index, axis=0))
    return combine(parts_out, parts_log, HD)


def solution(mesh):
    return jax.shard_map(
        per_device,
        mesh=mesh,
        in_specs=(
            P(("groups", "seq"), "tensor"),
            P(("groups", "seq"), "tensor"),
            P(("groups", "seq"), "tensor"),
            P(("groups", "seq"), "tensor"),
            P(("groups", "seq"), "tensor"),
            P(("groups", "seq"), None),
            P(("groups", "seq"), None),
            P("groups"),
        ),
        out_specs=P(("groups", "seq"), "tensor"),
        check_vma=False,
    )
```

profile of v0, /device:TPU:0, one launch (start us, length us, event | category | flops | bytes accessed | tf_op | source)
XLA Modules:
  0.0 122.4 jit_solution(11329820267524325412)
XLA Ops:
  0.0 0.8 reduce-window.4
  2.1 0.8 fusion.29
  3.2 5.5 %gather_fusion = bf16[320,2048]{1,0:T(8,128)(2,1)S(1)} fusion(bf16[128,2048]{1,0:T(8,128)(2,1)} %param.20, s32[1024]{0:T(1024)S(1)} %pad_clamp_fusion.2), kind=kCustom, calls=%fused_computation.4 | custom fusion | bytes 2622720 | tf_op jit(solution)/shard_map/jit(_take)/gather | solution.py:94
  8.7 1.3 %select_select_fusion = bf16[8,40,2048]{2,1,0:T(8,128)(2,1)} fusion(bf16[8,40,2048]{2,1,0:T(8,128)(2,1)S(1)} %bitcast.127, pred[8,40]{1,0:T(8,128)(4,1)S(1)} %get-tuple-element.153, pred[8,40]{1,0:T(8,128)(4,1)S(1)} %get-tuple-element.152), kind=kLoop, calls=%fused_computation.54 | loop fusion | flops 1310720 | bytes 2622080 | tf_op jit(solution)/shard_map/jit(_where)/select_n | solution.py:97
  10.0 7.3 %all-to-all-start = ((bf16[8,40,2048]{2,1,0:T(8,128)(2,1)}), bf16[8,40,2048]{2,1,0:T(8,128)(2,1)S(1)}, u32[]{:S(2)}, u32[]{:S(2)}) async-start(bf16[8,40,2048]{2,1,0:T(8,128)(2,1)} %select_select_fusion), calls=%async_computation | async-start | bytes 2621440 | tf_op jit(solution)/shard_map/all_to_all | solution.py:103
  17.5 31.2 %all-to-all-done = bf16[8,40,2048]{2,1,0:T(8,128)(2,1)S(1)} async-done(((bf16[8,40,2048]{2,1,0:T(8,128)(2,1)}), bf16[8,40,2048]{2,1,0:T(8,128)(2,1)S(1)}, u32[]{:S(2)}, u32[]{:S(2)}) %all-to-all-start) | async-done | bytes 1310752 | tf_op jit(solution)/shard_map/all_to_all | solution.py:103
  48.7 23.1 %while.25 = (s32[]{:T(128)}, bf16[5,64,2048]{2,1,0:T(8,128)(2,1)}, f32[5,64,16]{1,0,2:T(8,128)S(1)}, bf16[5,64,2048]{2,1,0:T(8,128)(2,1)S(1)}, bf16[1024,256]{1,...) while((s32[]{:T(128)}, bf16[5,64,2048]{2,1,0:T(8,128)(2,1)}, ...), condition=%wide.region_15.16_spmd, body=%wide.region_10.15_spmd.sunk | while | flops 545914880 | bytes 16838760 | solution.py:113
  52.6 0.7 maximum_dynamic-update-slice_fusion.2
  57.2 0.7 maximum_dynamic-update-slice_fusion.2
  61.8 0.7 maximum_dynamic-update-slice_fusion.2
  66.4 0.7 maximum_dynamic-update-slice_fusion.2
  71.1 0.7 maximum_dynamic-update-slice_fusion.2
  71.9 0.7 reshape.449
  72.7 3.6 %all-to-all-start.1 = ((f32[8,1,640]{2,1,0:T(1,128)}), f32[8,1,640]{2,1,0:T(1,128)S(1)}, u32[]{:S(2)}, u32[]{:S(2)}) async-start(f32[8,1,640]{2,1,0:T(1,128)} %reshape.449), calls=%async_computation.1 | async-start | bytes 40960 | tf_op jit(solution)/shard_map/all_to_all | solution.py:119
  76.4 6.5 %all-to-all-done.1 = f32[8,1,640]{2,1,0:T(1,128)S(1)} async-done(((f32[8,1,640]{2,1,0:T(1,128)}), f32[8,1,640]{2,1,0:T(1,128)S(1)}, u32[]{:S(2)}, u32[]{:S(2)}) %all-to-all-start.1) | async-done | bytes 20512 | tf_op jit(solution)/shard_map/all_to_all | solution.py:119
  82.9 3.6 %all-to-all-start.2 = ((bf16[8,40,2048]{2,1,0:T(8,128)(2,1)}), bf16[8,40,2048]{2,1,0:T(8,128)(2,1)S(1)}, u32[]{:S(2)}, u32[]{:S(2)}) async-start(bf16[8,40,2048]{2,1,0:T(8,128)(2,1)} %bitcast.131), calls=%async_computation.2 | async-start | bytes 2621440 | tf_op jit(solution)/shard_map/all_to_all | solution.py:116
  86.6 5.6 %while.24 = (s32[]{:T(128)}, f32[2,64,2048]{2,1,0:T(8,128)}, f32[2,64,16]{1,0,2:T(2,128)S(1)}, pred[2,64,128]{2,1,0:T(8,128)(4,1)S(1)}, bf16[2,64,2048]{2,1,0:T(...) while((s32[]{:T(128)}, f32[2,64,2048]{2,1,0:T(8,128)}, ...), condition=%wide.region_7.8_spmd, body=%wide.region_2.7_spmd.sunk | while | flops 68157440 | bytes 6574197 | solution.py:127
  88.5 0.9 fusion.76
  91.3 0.9 fusion.76
  94.4 9.9 %compare_and_fusion.2 = (pred[128]{0:T(512)(128)(4,1)S(1)}, s32[128]{0:T(128)S(1)}, pred[128]{0:T(512)(128)(4,1)S(1)}, s32[128]{0:T(128)S(1)}) fusion(s32[]{:T(128)} %bitcast.29, s32[]{:T(128)} %bitcast.28, s32[]{:T(128)} %bitcast.27, s32[]{:T(128)} %bitcast.26, s32[]{:T(128)} %bitcast.23, s32[]{:T(128)} %bitcast.22, s32[]{:T(128)} %bitcast.21, ...), kind=kLoop, calls=%fused_computation.103 | loop fusion | flops 10112 | bytes 1856 | tf_op jit(solution)/shard_map/jit(_take)/and | solution.py:138
  107.6 9.5 %all-to-all-done.2 = bf16[8,40,2048]{2,1,0:T(8,128)(2,1)S(1)} async-done(((bf16[8,40,2048]{2,1,0:T(8,128)(2,1)}), bf16[8,40,2048]{2,1,0:T(8,128)(2,1)S(1)}, u32[]{:S(2)}, u32[]{:S(2)}) %all-to-all-start.2) | async-done | bytes 1310752 | tf_op jit(solution)/shard_map/all_to_all | solution.py:116
  117.0 0.9 gather_fusion.3
  117.9 0.9 gather_fusion.4
  120.1 2.3 %fusion.24 = bf16[128,2048]{1,0:T(8,128)(2,1)} fusion(f32[16,8,16,128]{3,2,1,0:T(8,128)S(1)} %bitcast.128, f32[16,8,16,128]{3,2,1,0:T(8,128)S(1)} %bitcast.129, f32[16,8,16,128]{3,2,1,0:T(8,128)S(1)} %bitcast.130, f32[2,64,2048]{2,1,0:T(8,128)S(1)} %copy-done.5, bf16[128,2048]{1,0:T(8,128)(2,1)S(1)} %gather_fusion.4, bf16[128,2048]{1,0:T(8,128)(2,1)S(1)} %gather_fusion.3, ...), kind=kLoop, calls=%fused_computation.57 | loop fusion | flops 2621440 | bytes 5767424 | tf_op jit(solution)/shard_map/convert_element_type | solution.py:61
  (207 shorter events, 31.4 us)
Async XLA Ops:
  8.7 40.0 %copy-start.1 = (bf16[1024,256]{1,0:T(8,128)(2,1)S(1)}, bf16[1024,256]{1,0:T(8,128)(2,1)}, u32[]{:S(2)}) copy-start(bf16[1024,256]{1,0:T(8,128)(2,1)} %param.23) | copy-start | bytes 1572868
  8.7 40.0 %copy-start.2 = (bf16[1024,256]{1,0:T(8,128)(2,1)S(1)}, bf16[1024,256]{1,0:T(8,128)(2,1)}, u32[]{:S(2)}) copy-start(bf16[1024,256]{1,0:T(8,128)(2,1)} %param.24) | copy-start | bytes 1572868
  10.0 38.7 %all-to-all-start = ((bf16[8,40,2048]{2,1,0:T(8,128)(2,1)}), bf16[8,40,2048]{2,1,0:T(8,128)(2,1)S(1)}, u32[]{:S(2)}, u32[]{:S(2)}) async-start(bf16[8,40,2048]{2,1,0:T(8,128)(2,1)} %select_select_fusion), calls=%async_computation | async-start | bytes 2621440 | tf_op jit(solution)/shard_map/all_to_all | solution.py:103
  71.8 14.7 %copy-start = (bf16[128,2048]{1,0:T(8,128)(2,1)S(1)}, bf16[128,2048]{1,0:T(8,128)(2,1)}, u32[]{:S(2)}) copy-start(bf16[128,2048]{1,0:T(8,128)(2,1)} %param.20) | copy-start | bytes 1572868
  71.8 14.7 %copy-start.3 = (bf16[128,256]{1,0:T(8,128)(2,1)S(1)}, bf16[128,256]{1,0:T(8,128)(2,1)}, u32[]{:S(2)}) copy-start(bf16[128,256]{1,0:T(8,128)(2,1)} %param.22) | copy-start | bytes 196612
  71.8 14.7 %copy-start.4 = (bf16[128,256]{1,0:T(8,128)(2,1)S(1)}, bf16[128,256]{1,0:T(8,128)(2,1)}, u32[]{:S(2)}) copy-start(bf16[128,256]{1,0:T(8,128)(2,1)} %param.21) | copy-start | bytes 196612
  72.7 10.2 %all-to-all-start.1 = ((f32[8,1,640]{2,1,0:T(1,128)}), f32[8,1,640]{2,1,0:T(1,128)S(1)}, u32[]{:S(2)}, u32[]{:S(2)}) async-start(f32[8,1,640]{2,1,0:T(1,128)} %reshape.449), calls=%async_computation.1 | async-start | bytes 40960 | tf_op jit(solution)/shard_map/all_to_all | solution.py:119
  82.9 34.1 %all-to-all-start.2 = ((bf16[8,40,2048]{2,1,0:T(8,128)(2,1)}), bf16[8,40,2048]{2,1,0:T(8,128)(2,1)S(1)}, u32[]{:S(2)}, u32[]{:S(2)}) async-start(bf16[8,40,2048]{2,1,0:T(8,128)(2,1)} %bitcast.131), calls=%async_computation.2 | async-start | bytes 2621440 | tf_op jit(solution)/shard_map/all_to_all | solution.py:116
  86.5 5.8 %copy-start.8 = (s32[8]{0:T(128)S(1)}, s32[8]{0:T(128)}, u32[]{:S(2)}) copy-start(s32[8]{0:T(128)} %param.27) | copy-start | bytes 100
  86.5 5.9 %copy-start.6 = (s32[4,1]{0,1:T(1,128)S(1)}, s32[4,1]{0,1:T(1,128)}, u32[]{:S(2)}) copy-start(s32[4,1]{0,1:T(1,128)} %param.25) | copy-start | bytes 52
  86.5 6.5 %copy-start.7 = (s32[1,4]{1,0:T(1,128)S(1)}, s32[1,4]{1,0:T(1,128)}, u32[]{:S(2)}) copy-start(s32[1,4]{1,0:T(1,128)} %param.26) | copy-start | bytes 52
  118.9 1.2 %copy-start.5 = (f32[2,64,2048]{2,1,0:T(8,128)S(1)}, f32[2,64,2048]{2,1,0:T(8,128)}, u32[]{:S(2)}) copy-start(f32[2,64,2048]{2,1,0:T(8,128)} %get-tuple-element.82) | copy-start | bytes 3145732
where the time goes:
time: 123 us; the launch traced here: 122 us
  waiting for transfers between devices  47.1 us (38%)
  other arithmetic  28.8 us (23%)
  local copies, waits for them, and re-layouts  18.7 us (15%)
  starting transfers between devices  14.5 us (12%)
  matrix products  12.4 us (10%)
    all_to_all x1, waiting for transfers between devices, per_device(): lax.all_to_all(outgoing, 'seq', split_axis=0, concat_axis=0, tiled=True)  31.2 us
    and x1, other arithmetic, per_device(): parts_log.append(jnp.take(flat_log, flat_index, axis=0))  9.95 us
    all_to_all x1, waiting for transfers between devices, per_device(): lax.all_to_all(as_sent(part_out), 'seq', split_axis=0, concat_axis=0, til...  9.46 us
    all_to_all x1, starting transfers between devices, per_device(): lax.all_to_all(outgoing, 'seq', split_axis=0, concat_axis=0, tiled=True)  7.28 us
    all_to_all x1, waiting for transfers between devices, per_device(): lax.all_to_all(part_log, 'seq', split_axis=0, concat_axis=0, tiled=True)  6.48 us
    dot_general x14, matrix products, attend(): result = jnp.dot(weights, value_part, preferred_element_type=jnp.float32)  6.29 us
    dot_general x14, matrix products, attend(): lax.dot_general(query_rows, key_part, (((1,), (1,)), ((), ())), preferred...  6.08 us
    reduce_sum x14, other arithmetic, attend(): summed = jnp.sum(jnp.exp(scores - highest), axis=1, keepdims=True)  5.6 us
  transfers between devices with their start and end apart: 3, of which 3 were waited for; matrix products, arithmetic and copies ran while one was open for 17% of the time, Pallas kernels for 0%

commit v1 on v0

v1 whole, which is shorter than its diff:
```python
import functools
import math

import jax
import jax.numpy as jnp
from jax import lax
from jax.experimental import pallas as pl
from jax.experimental.pallas import tpu as pltpu
from jax.sharding import PartitionSpec as P

HD = 128
PROMPTS = 4
LEN_MOST = 40
LANES = 128
GROUPS_OF_8 = LEN_MOST // 8
LOG2E = 1.4426950408889634
MESH = pl.DeviceIdType.MESH

F32 = jnp.float32
BF16 = jnp.bfloat16


def xor(a, b, n):
    total = 0
    bit = 1
    while bit < n:
        total = total + bit * (((a // bit) % 2 + (b // bit) % 2) % 2)
        bit *= 2
    return total


def nt_dot(a, b):
    return lax.dot_general(a, b, (((1,), (1,)), ((), ())), preferred_element_type=F32)


def kernel(
    n,
    order_ref,
    prompt_ref,
    len_ref,
    q_ref,
    rk_ref,
    rv_ref,
    pk_ref,
    pv_ref,
    out_ref,
    send_q,
    recv_q,
    send_o,
    recv_o,
    send_l,
    recv_l,
    v_ext,
    rv_ext,
    local_o,
    local_l,
    q_send_sem,
    q_recv_sem,
    o_send_sem,
    o_recv_sem,
    l_send_sem,
    l_recv_sem,
):
    me = lax.axis_index("seq")
    shards = n // PROMPTS
    tok = q_ref.shape[0]
    kv_heads = rk_ref.shape[1] // HD
    heads = q_ref.shape[1] // HD
    per_kv = heads // kv_heads
    rows = per_kv * LEN_MOST
    resp = prompt_ref.shape[0]
    power = LOG2E / math.sqrt(HD)

    def peer_of(step):
        return xor(me, step, n) if n & (n - 1) == 0 else lax.rem(me + step, n)

    def giver_of(step):
        return xor(me, step, n) if n & (n - 1) == 0 else lax.rem(me + n - step, n)

    barrier = pltpu.get_barrier_semaphore()

    def greet(step, carry):
        pl.semaphore_signal(
            barrier, inc=1, device_id={"seq": peer_of(step)}, device_id_type=MESH
        )
        return carry

    lax.fori_loop(1, n, greet, 0)

    lengths = [len_ref[0, k] for k in range(resp)]
    prompts = [prompt_ref[k, 0] for k in range(resp)]
    starts = [jnp.int32(0)]
    for k in range(resp - 1):
        starts.append(starts[-1] + lengths[k])

    def placed(d):
        rank = order_ref[d]
        first = jnp.int32(0)
        live = jnp.int32(0)
        which = jnp.int32(0)
        for k in range(resp):
            low = prompts[k] * shards
            hit = (rank >= low) & (rank < low + shards)
            first = jnp.where(hit, starts[k], first)
            live = jnp.where(hit, lengths[k], live)
            which = jnp.where(hit, rank - low, which)
        return first, live, which

    slot = lax.broadcasted_iota(jnp.int32, (LEN_MOST, tok), 0)
    token = lax.broadcasted_iota(jnp.int32, (LEN_MOST, tok), 1)

    def gather_block(d):
        first, live, _ = placed(d)
        chosen = ((token == first + slot) & (slot < live)).astype(F32).astype(BF16)
        picked = jnp.dot(chosen, q_ref[...], preferred_element_type=F32)
        for g in range(kv_heads):
            parts = [
                picked[:, (g * per_kv + h) * HD : (g * per_kv + h + 1) * HD] for h in range(per_kv)
            ]
            send_q[d, g] = jnp.concatenate(parts, axis=0).astype(BF16)

    def q_copy(slot_from, slot_to, peer):
        return pltpu.make_async_remote_copy(
            src_ref=send_q.at[slot_from],
            dst_ref=recv_q.at[slot_to],
            send_sem=q_send_sem.at[slot_from],
            recv_sem=q_recv_sem.at[slot_to],
            device_id={"seq": peer},
            device_id_type=MESH,
        )

    def o_copy(slot_from, slot_to, peer):
        return pltpu.make_async_remote_copy(
            src_ref=send_o.at[slot_from],
            dst_ref=recv_o.at[slot_to],
            send_sem=o_send_sem.at[slot_from],
            recv_sem=o_recv_sem.at[slot_to],
            device_id={"seq": peer},
            device_id_type=MESH,
        )

    def l_copy(slot_from, slot_to, peer):
        return pltpu.make_async_remote_copy(
            src_ref=send_l.at[slot_from],
            dst_ref=recv_l.at[slot_to],
            send_sem=l_send_sem.at[slot_from],
            recv_sem=l_recv_sem.at[slot_to],
            device_id={"seq": peer},
            device_id_type=MESH,
        )

    pl.semaphore_wait(barrier, n - 1)

    def send_step(i, carry):
        peer = peer_of(n - 1 - i)
        gather_block(peer)
        q_copy(peer, me, peer).start()
        return carry

    lax.fori_loop(0, n - 1, send_step, 0)
    gather_block(me)

    ones = jnp.ones((pk_ref.shape[0], HD), BF16)
    for g in range(kv_heads):
        v_ext[g] = jnp.concatenate([pv_ref[:, g * HD : (g + 1) * HD], ones], axis=1)
    ones = jnp.ones((tok, HD), BF16)
    for g in range(kv_heads):
        rv_ext[g] = jnp.concatenate([rv_ref[:, g * HD : (g + 1) * HD], ones], axis=1)

    lane8 = lax.broadcasted_iota(jnp.int32, (8, LANES), 1)

    def owner_block(q_block, g):
        scores = nt_dot(q_block, pk_ref[:, g * HD : (g + 1) * HD])
        highest = jnp.max(scores, axis=1, keepdims=True)
        weights = jnp.exp2((scores - highest) * power).astype(BF16)
        both = jnp.dot(weights, v_ext[g], preferred_element_type=F32)
        total = both[:, HD:]
        return (both[:, :HD] / total).astype(BF16), highest * power + jnp.log2(total)

    def packed_logs(logs):
        packed = jnp.zeros((8, LANES), F32)
        for g in range(kv_heads):
            for h in range(per_kv):
                for k in range(GROUPS_OF_8):
                    row = h * LEN_MOST + k * 8
                    packed = jnp.where(
                        lane8 == k * heads + g * per_kv + h, logs[g][row : row + 8, :], packed
                    )
        return packed

    def own_block():
        logs = []
        for g in range(kv_heads):
            result, log_part = owner_block(send_q[me, g], g)
            recv_o[me, g] = result
            logs.append(log_part)
        recv_l[me] = packed_logs(logs)

    def serve(step, carry):
        peer = giver_of(step)
        q_copy(peer, peer, peer).wait_recv()
        logs = []
        for g in range(kv_heads):
            result, log_part = owner_block(recv_q[peer, g], g)
            send_o[peer, g] = result
            logs.append(log_part)
        send_l[peer] = packed_logs(logs)
        o_copy(peer, me, peer).start()
        l_copy(peer, me, peer).start()
        return carry

    own_block()

    row_id = lax.broadcasted_iota(jnp.int32, (tok, tok), 0)
    col_id = lax.broadcasted_iota(jnp.int32, (tok, tok), 1)
    begin = jnp.zeros((tok, tok), jnp.int32)
    for k in range(1, resp):
        begin = jnp.where(row_id >= starts[k], starts[k], begin)
    allowed = (col_id >= begin) & (col_id <= row_id)
    lane_tok = lax.broadcasted_iota(jnp.int32, (tok, LANES), 1)

    local_log = jnp.zeros((tok, LANES), F32)
    for h in range(heads):
        g = h // per_kv
        scores = nt_dot(q_ref[:, h * HD : (h + 1) * HD], rk_ref[:, g * HD : (g + 1) * HD])
        scores = jnp.where(allowed, scores, -1e30)
        highest = jnp.max(scores, axis=1, keepdims=True)
        weights = jnp.exp2((scores - highest) * power).astype(BF16)
        both = jnp.dot(weights, rv_ext[g], preferred_element_type=F32)
        total = both[:, HD:]
        local_o[h] = both[:, :HD] / total
        local_log = jnp.where(lane_tok == h, highest * power + jnp.log2(total), local_log)
    local_l[...] = local_log

    lax.fori_loop(1, n, serve, 0)

    column = lax.broadcasted_iota(jnp.int32, (8, n * LEN_MOST), 1)
    targets = [jnp.full((8, n * LEN_MOST), -1, jnp.int32) for _ in range(shards)]
    for d in range(n):
        first, live, which = placed(d)
        place = column - d * LEN_MOST
        here = (place >= 0) & (place < live)
        for j in range(shards):
            targets[j] = jnp.where(here & (which == j), place + first, targets[j])
    token_row = lax.broadcasted_iota(jnp.int32, (tok, n * LEN_MOST), 0)
    chosen = [
        (token_row == jnp.broadcast_to(t[0:1, :], (tok, n * LEN_MOST))).astype(F32).astype(BF16)
        for t in targets
    ]
    chosen = jnp.concatenate(chosen, axis=0)

    def receive(step, carry):
        peer = giver_of(step)
        o_copy(peer, peer, peer).wait_recv()
        l_copy(peer, peer, peer).wait_recv()
        return carry

    lax.fori_loop(1, n, receive, 0)

    log_rows = []
    for d in range(n):
        packed = recv_l[d]
        for k in range(GROUPS_OF_8):
            log_rows.append(pltpu.roll(packed, LANES - k * heads, 1) if k else packed)
    log_all = jnp.concatenate(log_rows, axis=0)
    high = log_all.astype(BF16)
    rest = log_all - high.astype(F32)
    middle = rest.astype(BF16)
    low = (rest - middle.astype(F32)).astype(BF16)
    logs = jnp.dot(chosen, high, preferred_element_type=F32)
    logs = logs + jnp.dot(chosen, middle, preferred_element_type=F32)
    logs = logs + jnp.dot(chosen, low, preferred_element_type=F32)
    parts_log = [local_l[...]] + [logs[j * tok : (j + 1) * tok] for j in range(shards)]
    highest = functools.reduce(jnp.maximum, parts_log)
    shares = [jnp.exp2(part - highest) for part in parts_log]
    inverse = 1.0 / functools.reduce(jnp.add, shares)
    shares = [share * inverse for share in shares]

    for g in range(kv_heads):
        wide = [recv_o[d, g].astype(F32) for d in range(n)]
        for h in range(per_kv):
            head = g * per_kv + h
            stacked = jnp.concatenate(
                [w[h * LEN_MOST : (h + 1) * LEN_MOST] for w in wide], axis=0
            ).astype(BF16)
            taken = jnp.dot(chosen, stacked, preferred_element_type=F32)
            blended = shares[0][:, head : head + 1] * local_o[head]
            for j in range(shards):
                blended = blended + (
                    shares[j + 1][:, head : head + 1] * taken[j * tok : (j + 1) * tok]
                )
            out_ref[:, head * HD : (head + 1) * HD] = blended.astype(BF16)

    def finish(step, carry):
        peer = peer_of(step)
        q_copy(peer, me, peer).wait_send()
        o_copy(peer, me, peer).wait_send()
        l_copy(peer, me, peer).wait_send()
        return carry

    lax.fori_loop(1, n, finish, 0)


def per_device(
    queries,
    resp_keys,
    resp_values,
    prompt_keys,
    prompt_values,
    response_prompt,
    response_lengths,
    shard_order,
):
    n = lax.axis_size("seq")
    tok = queries.shape[0]
    kv_heads = resp_keys.shape[1] // HD
    heads = queries.shape[1] // HD
    rows = heads // kv_heads * LEN_MOST
    keys = prompt_keys.shape[0]
    block = (n, kv_heads, rows, HD)
    smem = pl.BlockSpec(memory_space=pltpu.SMEM)
    vmem = pl.BlockSpec(memory_space=pltpu.VMEM)
    return pl.pallas_call(
        functools.partial(kernel, n),
        out_shape=jax.ShapeDtypeStruct(queries.shape, BF16),
        in_specs=[smem] * 3 + [vmem] * 5,
        out_specs=vmem,
        scratch_shapes=[
            pltpu.VMEM(block, BF16),
            pltpu.VMEM(block, BF16),
            pltpu.VMEM(block, BF16),
            pltpu.VMEM(block, BF16),
            pltpu.VMEM((n, 8, LANES), F32),
            pltpu.VMEM((n, 8, LANES), F32),
            pltpu.VMEM((kv_heads, keys, 2 * HD), BF16),
            pltpu.VMEM((kv_heads, tok, 2 * HD), BF16),
            pltpu.VMEM((heads, tok, HD), F32),
            pltpu.VMEM((tok, LANES), F32),
        ]
        + [pltpu.SemaphoreType.DMA((n,))] * 6,
        compiler_params=pltpu.CompilerParams(
            collective_id=0, has_side_effects=True, vmem_limit_bytes=56 * 1024 * 1024
        ),
    )(
        shard_order,
        response_prompt,
        response_lengths,
        queries,
        resp_keys,
        resp_values,
        prompt_keys,
        prompt_values,
    )


def solution(mesh):
    return jax.shard_map(
        per_device,
        mesh=mesh,
        in_specs=(
            P(("groups", "seq"), "tensor"),
            P(("groups", "seq"), "tensor"),
            P(("groups", "seq"), "tensor"),
            P(("groups", "seq"), "tensor"),
            P(("groups", "seq"), "tensor"),
            P(("groups", "seq"), None),
            P(("groups", "seq"), None),
            P("groups"),
        ),
        out_specs=P(("groups", "seq"), "tensor"),
        check_vma=False,
    )
```

time: 123 us -> 70.7 us (0.57)
  the two profiles are of different devices: /device:TPU:0 before, /device:TPU:9 now
where the time goes in v1:
time: 70.7 us; the launch traced here: 70.5 us
  Pallas kernels  67.3 us (95%)
  local copies, waits for them, and re-layouts  3.19 us (5%)
    pallas_call x1, Pallas kernels, per_device(): pl.pallas_call(functools.partial(kernel, n), out_shape=jax.ShapeDtypeStru...  67.3 us
    unnamed x2, local copies, waits for them, and re-layouts  3.19 us

profile of v1, /device:TPU:9, one launch (start us, length us, event | category | flops | bytes accessed | tf_op | source)
XLA Modules:
  0.0 70.5 jit_solution(7051176429234271640)
XLA Ops:
  0.0 1.3 %copy.9.prompt_ref = s32[4,1]{1,0:T(4,128)} copy(s32[4,1]{0,1:T(1,128)} %param.13) | data formatting | bytes 32 | tf_op args[5]
  1.3 67.3 %shard_map.82 = bf16[128,2048]{1,0:T(8,128)(2,1)} custom-call(s32[8]{0:T(128)} %order_ref.1, s32[4,1]{1,0:T(4,128)} %copy.9.prompt_ref, s32[1,4]{1,0:T(1,128)} %len_ref.1, bf16[128,2048]{1,0:T(8,128)(2,1)} %q_ref.1, bf16[128,256]{1,0:T(8,128)(2,1)} %rk_ref.1, bf16[128,256]{1,0:T(8,128)(2,1)} %rv_ref.1, bf16[1024,256]{1,0:T(8,128)(2,1)} %pk_ref.1, ...), custom_call_target="tpu_custom_call" | custom-call | tf_op jit(solution)/shard_map/pallas_call | solution.py:323
  68.7 1.9 %copy.11 = bf16[128,2048]{1,0:T(8,128)(2,1)} copy(bf16[128,2048]{1,0:T(8,128)(2,1)} %shard_map.82) | data formatting | bytes 1048576

commit v2 on v1

--- a/solution.py
+++ b/solution.py
@@ -50,6 +50,7 @@
     recv_o,
     send_l,
     recv_l,
+    far_kv,
     v_ext,
     rv_ext,
     local_o,
@@ -60,28 +61,25 @@
     o_recv_sem,
     l_send_sem,
     l_recv_sem,
+    kv_send_sem,
+    kv_recv_sem,
 ):
     me = lax.axis_index("seq")
+    half = n // 2
+    mate = xor(me, half, n)
     shards = n // PROMPTS
     tok = q_ref.shape[0]
     kv_heads = rk_ref.shape[1] // HD
     heads = q_ref.shape[1] // HD
     per_kv = heads // kv_heads
-    rows = per_kv * LEN_MOST
     resp = prompt_ref.shape[0]
     power = LOG2E / math.sqrt(HD)
 
-    def peer_of(step):
-        return xor(me, step, n) if n & (n - 1) == 0 else lax.rem(me + step, n)
-
-    def giver_of(step):
-        return xor(me, step, n) if n & (n - 1) == 0 else lax.rem(me + n - step, n)
-
     barrier = pltpu.get_barrier_semaphore()
 
     def greet(step, carry):
         pl.semaphore_signal(
-            barrier, inc=1, device_id={"seq": peer_of(step)}, device_id_type=MESH
+            barrier, inc=1, device_id={"seq": xor(me, step, n)}, device_id_type=MESH
         )
         return carry
 
@@ -106,12 +104,12 @@
             which = jnp.where(hit, rank - low, which)
         return first, live, which
 
-    slot = lax.broadcasted_iota(jnp.int32, (LEN_MOST, tok), 0)
-    token = lax.broadcasted_iota(jnp.int32, (LEN_MOST, tok), 1)
+    slot_id = lax.broadcasted_iota(jnp.int32, (LEN_MOST, tok), 0)
+    token_id = lax.broadcasted_iota(jnp.int32, (LEN_MOST, tok), 1)
 
     def gather_block(d):
         first, live, _ = placed(d)
-        chosen = ((token == first + slot) & (slot < live)).astype(F32).astype(BF16)
+        chosen = ((token_id == first + slot_id) & (slot_id < live)).astype(F32).astype(BF16)
         picked = jnp.dot(chosen, q_ref[...], preferred_element_type=F32)
         for g in range(kv_heads):
             parts = [
@@ -119,45 +117,67 @@
             ]
             send_q[d, g] = jnp.concatenate(parts, axis=0).astype(BF16)
 
-    def q_copy(slot_from, slot_to, peer):
+    def q_copy(d, g, giver, slot, peer):
         return pltpu.make_async_remote_copy(
-            src_ref=send_q.at[slot_from],
-            dst_ref=recv_q.at[slot_to],
-            send_sem=q_send_sem.at[slot_from],
-            recv_sem=q_recv_sem.at[slot_to],
+            src_ref=send_q.at[d, g],
+            dst_ref=recv_q.at[giver, slot],
+            send_sem=q_send_sem.at[d, g],
+            recv_sem=q_recv_sem.at[giver, slot],
             device_id={"seq": peer},
             device_id_type=MESH,
         )
 
-    def o_copy(slot_from, slot_to, peer):
+    def o_copy(giver, slot, d, g, peer):
         return pltpu.make_async_remote_copy(
-            src_ref=send_o.at[slot_from],
-            dst_ref=recv_o.at[slot_to],
-            send_sem=o_send_sem.at[slot_from],
-            recv_sem=o_recv_sem.at[slot_to],
+            src_ref=send_o.at[giver, slot],
+            dst_ref=recv_o.at[d, g],
+            send_sem=o_send_sem.at[giver, slot],
+            recv_sem=o_recv_sem.at[d, g],
             device_id={"seq": peer},
             device_id_type=MESH,
         )
 
-    def l_copy(slot_from, slot_to, peer):
+    def l_copy(giver, slot, d, g, peer):
         return pltpu.make_async_remote_copy(
-            src_ref=send_l.at[slot_from],
-            dst_ref=recv_l.at[slot_to],
-            send_sem=l_send_sem.at[slot_from],
-            recv_sem=l_recv_sem.at[slot_to],
+            src_ref=send_l.at[giver, slot],
+            dst_ref=recv_l.at[d, g],
+            send_sem=l_send_sem.at[giver, slot],
+            recv_sem=l_recv_sem.at[d, g],
             device_id={"seq": peer},
             device_id_type=MESH,
         )
 
+    def kv_copy(which):
+        source = (pk_ref, pv_ref)[which]
+        return pltpu.make_async_remote_copy(
+            src_ref=source.at[:, pl.ds(HD, HD)],
+            dst_ref=far_kv.at[which],
+            send_sem=kv_send_sem.at[which],
+            recv_sem=kv_recv_sem.at[which],
+            device_id={"seq": mate},
+            device_id_type=MESH,
+        )
+
     pl.semaphore_wait(barrier, n - 1)
 
-    def send_step(i, carry):
-        peer = peer_of(n - 1 - i)
+    def send_far(step, carry):
+        peer = xor(me, step, n)
         gather_block(peer)
-        q_copy(peer, me, peer).start()
-        return carry
-
-    lax.fori_loop(0, n - 1, send_step, 0)
+        q_copy(peer, 0, me, 0, peer).start()
+        return carry
+
+    def send_near(step, carry):
+        peer = xor(me, step, n)
+        gather_block(peer)
+        q_copy(peer, 0, me, 0, peer).start()
+        q_copy(peer, 1, me, 1, peer).start()
+        q_copy(xor(peer, half, n), 1, me, 2, peer).start()
+        return carry
+
+    kv_copy(0).start()
+    kv_copy(1).start()
+    lax.fori_loop(half, n, send_far, 0)
+    lax.fori_loop(1, half, send_near, 0)
     gather_block(me)
 
     ones = jnp.ones((pk_ref.shape[0], HD), BF16)
@@ -169,47 +189,52 @@
 
     lane8 = lax.broadcasted_iota(jnp.int32, (8, LANES), 1)
 
-    def owner_block(q_block, g):
-        scores = nt_dot(q_block, pk_ref[:, g * HD : (g + 1) * HD])
+    def owner_block(q_block, g, far=False):
+        keys = far_kv[0] if far else pk_ref[:, g * HD : (g + 1) * HD]
+        scores = nt_dot(q_block, keys)
         highest = jnp.max(scores, axis=1, keepdims=True)
         weights = jnp.exp2((scores - highest) * power).astype(BF16)
-        both = jnp.dot(weights, v_ext[g], preferred_element_type=F32)
+        both = jnp.dot(weights, v_ext[kv_heads if far else g], preferred_element_type=F32)
         total = both[:, HD:]
-        return (both[:, :HD] / total).astype(BF16), highest * power + jnp.log2(total)
-
-    def packed_logs(logs):
+        logs = highest * power + jnp.log2(total)
         packed = jnp.zeros((8, LANES), F32)
-        for g in range(kv_heads):
-            for h in range(per_kv):
-                for k in range(GROUPS_OF_8):
-                    row = h * LEN_MOST + k * 8
-                    packed = jnp.where(
-                        lane8 == k * heads + g * per_kv + h, logs[g][row : row + 8, :], packed
-                    )
-        return packed
-
-    def own_block():
-        logs = []
-        for g in range(kv_heads):
-            result, log_part = owner_block(send_q[me, g], g)
-            recv_o[me, g] = result
-            logs.append(log_part)
-        recv_l[me] = packed_logs(logs)
-
-    def serve(step, carry):
-        peer = giver_of(step)
-        q_copy(peer, peer, peer).wait_recv()
-        logs = []
-        for g in range(kv_heads):
-            result, log_part = owner_block(recv_q[peer, g], g)
-            send_o[peer, g] = result
-            logs.append(log_part)
-        send_l[peer] = packed_logs(logs)
-        o_copy(peer, me, peer).start()
-        l_copy(peer, me, peer).start()
-        return carry
-
-    own_block()
+        for h in range(per_kv):
+            for k in range(GROUPS_OF_8):
+                row = h * LEN_MOST + k * 8
+                packed = jnp.where(
+                    lane8 == k * heads + g * per_kv + h, logs[row : row + 8, :], packed
+                )
+        return (both[:, :HD] / total).astype(BF16), packed
+
+    def serve(giver, slot):
+        g = min(slot, 1)
+        owner = mate if slot == 2 else me
+        q_copy(giver, g, giver, slot, giver).wait_recv()
+        send_o[giver, slot], send_l[giver, slot] = owner_block(recv_q[giver, slot], g, slot == 2)
+        return (
+            o_copy(giver, slot, owner, g, giver),
+            l_copy(giver, slot, owner, g, giver),
+        )
+
+    def serve_near(step, carry):
+        giver = xor(me, step, n)
+        for slot in range(2):
+            for copy in serve(giver, slot):
+                copy.start()
+        return carry
+
+    def serve_far(step, carry):
+        for copy in serve(xor(me, step, n), 0):
+            copy.start()
+        return carry
+
+    def serve_mate(step, carry):
+        for copy in serve(xor(me, step, n), 2):
+            copy.start()
+        return carry
+
+    for g in range(kv_heads):
+        recv_o[me, g], recv_l[me, g] = owner_block(send_q[me, g], g)
 
     row_id = lax.broadcasted_iota(jnp.int32, (tok, tok), 0)
     col_id = lax.broadcasted_iota(jnp.int32, (tok, tok), 1)
@@ -232,7 +257,13 @@
         local_log = jnp.where(lane_tok == h, highest * power + jnp.log2(total), local_log)
     local_l[...] = local_log
 
-    lax.fori_loop(1, n, serve, 0)
+    lax.fori_loop(1, half, serve_near, 0)
+    lax.fori_loop(half, n, serve_far, 0)
+    for which in range(2):
+        kv_copy(which).wait_recv()
+    v_ext[kv_heads] = jnp.concatenate([far_kv[1], jnp.ones((pk_ref.shape[0], HD), BF16)], axis=1)
+    lax.fori_loop(1, half, serve_mate, 0)
+    recv_o[mate, 1], recv_l[mate, 1] = owner_block(send_q[mate, 1], 1, True)
 
     column = lax.broadcasted_iota(jnp.int32, (8, n * LEN_MOST), 1)
     targets = [jnp.full((8, n * LEN_MOST), -1, jnp.int32) for _ in range(shards)]
@@ -249,17 +280,27 @@
     ]
     chosen = jnp.concatenate(chosen, axis=0)
 
-    def receive(step, carry):
-        peer = giver_of(step)
-        o_copy(peer, peer, peer).wait_recv()
-        l_copy(peer, peer, peer).wait_recv()
-        return carry
-
-    lax.fori_loop(1, n, receive, 0)
+    def receive(d, g):
+        o_copy(d, g, d, g, d).wait_recv()
+        l_copy(d, g, d, g, d).wait_recv()
+
+    def receive_near(step, carry):
+        peer = xor(me, step, n)
+        receive(peer, 0)
+        receive(peer, 1)
+        receive(xor(peer, half, n), 1)
+        return carry
+
+    def receive_far(step, carry):
+        receive(xor(me, step, n), 0)
+        return carry
+
+    lax.fori_loop(half, n, receive_far, 0)
+    lax.fori_loop(1, half, receive_near, 0)
 
     log_rows = []
     for d in range(n):
-        packed = recv_l[d]
+        packed = recv_l[d, 0] + recv_l[d, 1]
         for k in range(GROUPS_OF_8):
             log_rows.append(pltpu.roll(packed, LANES - k * heads, 1) if k else packed)
     log_all = jnp.concatenate(log_rows, axis=0)
@@ -291,14 +332,27 @@
                 )
             out_ref[:, head * HD : (head + 1) * HD] = blended.astype(BF16)
 
-    def finish(step, carry):
-        peer = peer_of(step)
-        q_copy(peer, me, peer).wait_send()
-        o_copy(peer, me, peer).wait_send()
-        l_copy(peer, me, peer).wait_send()
-        return carry
-
-    lax.fori_loop(1, n, finish, 0)
+    def finish_near(step, carry):
+        peer = xor(me, step, n)
+        q_copy(peer, 0, me, 0, peer).wait_send()
+        q_copy(peer, 1, me, 1, peer).wait_send()
+        q_copy(xor(peer, half, n), 1, me, 2, peer).wait_send()
+        for slot in range(3):
+            o_copy(peer, slot, me, 0, peer).wait_send()
+            l_copy(peer, slot, me, 0, peer).wait_send()
+        return carry
+
+    def finish_far(step, carry):
+        peer = xor(me, step, n)
+        q_copy(peer, 0, me, 0, peer).wait_send()
+        o_copy(peer, 0, me, 0, peer).wait_send()
+        l_copy(peer, 0, me, 0, peer).wait_send()
+        return carry
+
+    for which in range(2):
+        kv_copy(which).wait_send()
+    lax.fori_loop(1, half, finish_near, 0)
+    lax.fori_loop(half, n, finish_far, 0)
 
 
 def per_device(
@@ -318,6 +372,7 @@
     rows = heads // kv_heads * LEN_MOST
     keys = prompt_keys.shape[0]
     block = (n, kv_heads, rows, HD)
+    slots = (n, 3, rows, HD)
     smem = pl.BlockSpec(memory_space=pltpu.SMEM)
     vmem = pl.BlockSpec(memory_space=pltpu.VMEM)
     return pl.pallas_call(
@@ -327,17 +382,25 @@
         out_specs=vmem,
         scratch_shapes=[
             pltpu.VMEM(block, BF16),
+            pltpu.VMEM(slots, BF16),
+            pltpu.VMEM(slots, BF16),
             pltpu.VMEM(block, BF16),
-            pltpu.VMEM(block, BF16),
-            pltpu.VMEM(block, BF16),
-            pltpu.VMEM((n, 8, LANES), F32),
-            pltpu.VMEM((n, 8, LANES), F32),
-            pltpu.VMEM((kv_heads, keys, 2 * HD), BF16),
+            pltpu.VMEM((n, 3, 8, LANES), F32),
+            pltpu.VMEM((n, kv_heads, 8, LANES), F32),
+            pltpu.VMEM((2, keys, HD), BF16),
+            pltpu.VMEM((kv_heads + 1, keys, 2 * HD), BF16),
             pltpu.VMEM((kv_heads, tok, 2 * HD), BF16),
             pltpu.VMEM((heads, tok, HD), F32),
             pltpu.VMEM((tok, LANES), F32),
-        ]
-        + [pltpu.SemaphoreType.DMA((n,))] * 6,
+            pltpu.SemaphoreType.DMA((n, kv_heads)),
+            pltpu.SemaphoreType.DMA((n, 3)),
+            pltpu.SemaphoreType.DMA((n, 3)),
+            pltpu.SemaphoreType.DMA((n, kv_heads)),
+            pltpu.SemaphoreType.DMA((n, 3)),
+            pltpu.SemaphoreType.DMA((n, kv_heads)),
+            pltpu.SemaphoreType.DMA((2,)),
+            pltpu.SemaphoreType.DMA((2,)),
+        ],
         compiler_params=pltpu.CompilerParams(
             collective_id=0, has_side_effects=True, vmem_limit_bytes=56 * 1024 * 1024
         ),

time: 70.7 us -> 67.8 us (0.959)
  the two profiles are of different devices: /device:TPU:9 before, /device:TPU:0 now
where the time goes in v2:
time: 67.8 us; the launch traced here: 67.6 us
  Pallas kernels  64.4 us (95%)
  local copies, waits for them, and re-layouts  3.19 us (5%)
    pallas_call x1, Pallas kernels, per_device(): pl.pallas_call(functools.partial(kernel, n), out_shape=jax.ShapeDtypeStru...  64.4 us
    unnamed x2, local copies, waits for them, and re-layouts  3.19 us

profile of v2, /device:TPU:0, one launch (start us, length us, event | category | flops | bytes accessed | tf_op | source)
XLA Modules:
  0.0 67.6 jit_solution(9910692768504130133)
XLA Ops:
  0.0 1.3 %copy.9.prompt_ref = s32[4,1]{1,0:T(4,128)} copy(s32[4,1]{0,1:T(1,128)} %param.13) | data formatting | bytes 32 | tf_op args[5]
  1.3 64.4 %shard_map.82 = bf16[128,2048]{1,0:T(8,128)(2,1)} custom-call(s32[8]{0:T(128)} %order_ref.1, s32[4,1]{1,0:T(4,128)} %copy.9.prompt_ref, s32[1,4]{1,0:T(1,128)} %len_ref.1, bf16[128,2048]{1,0:T(8,128)(2,1)} %q_ref.1, bf16[128,256]{1,0:T(8,128)(2,1)} %rk_ref.1, bf16[128,256]{1,0:T(8,128)(2,1)} %rv_ref.1, bf16[1024,256]{1,0:T(8,128)(2,1)} %pk_ref.1, ...), custom_call_target="tpu_custom_call" | custom-call | tf_op jit(solution)/shard_map/pallas_call | solution.py:378
  65.8 1.9 %copy.11 = bf16[128,2048]{1,0:T(8,128)(2,1)} copy(bf16[128,2048]{1,0:T(8,128)(2,1)} %shard_map.82) | data formatting | bytes 1048576

commit v3 on v2

--- a/solution.py
+++ b/solution.py
@@ -38,12 +38,18 @@
     order_ref,
     prompt_ref,
     len_ref,
+    q_hbm,
+    rk_hbm,
+    rv_hbm,
+    pk_hbm,
+    pv_hbm,
+    out_ref,
     q_ref,
     rk_ref,
     rv_ref,
     pk_ref,
     pv_ref,
-    out_ref,
+    load_sem,
     send_q,
     recv_q,
     send_o,
@@ -72,7 +78,7 @@
     kv_heads = rk_ref.shape[1] // HD
     heads = q_ref.shape[1] // HD
     per_kv = heads // kv_heads
-    resp = prompt_ref.shape[0]
+    resp = prompt_ref.shape[1]
     power = LOG2E / math.sqrt(HD)
 
     barrier = pltpu.get_barrier_semaphore()
@@ -85,8 +91,23 @@
 
     lax.fori_loop(1, n, greet, 0)
 
+    loads = [
+        pltpu.make_async_copy(source, target, load_sem.at[i])
+        for i, (source, target) in enumerate(
+            (
+                (q_hbm, q_ref),
+                (pk_hbm, pk_ref),
+                (pv_hbm, pv_ref),
+                (rk_hbm, rk_ref),
+                (rv_hbm, rv_ref),
+            )
+        )
+    ]
+    for load in loads:
+        load.start()
+
     lengths = [len_ref[0, k] for k in range(resp)]
-    prompts = [prompt_ref[k, 0] for k in range(resp)]
+    prompts = [prompt_ref[0, k] for k in range(resp)]
     starts = [jnp.int32(0)]
     for k in range(resp - 1):
         starts.append(starts[-1] + lengths[k])
@@ -148,7 +169,7 @@
         )
 
     def kv_copy(which):
-        source = (pk_ref, pv_ref)[which]
+        source = (pk_hbm, pv_hbm)[which]
         return pltpu.make_async_remote_copy(
             src_ref=source.at[:, pl.ds(HD, HD)],
             dst_ref=far_kv.at[which],
@@ -158,11 +179,12 @@
             device_id_type=MESH,
         )
 
-    pl.semaphore_wait(barrier, n - 1)
+    def gather_far(step, carry):
+        gather_block(xor(me, step, n))
+        return carry
 
     def send_far(step, carry):
         peer = xor(me, step, n)
-        gather_block(peer)
         q_copy(peer, 0, me, 0, peer).start()
         return carry
 
@@ -174,11 +196,16 @@
         q_copy(xor(peer, half, n), 1, me, 2, peer).start()
         return carry
 
+    loads[0].wait()
+    lax.fori_loop(half, n, gather_far, 0)
+    pl.semaphore_wait(barrier, n - 1)
     kv_copy(0).start()
     kv_copy(1).start()
     lax.fori_loop(half, n, send_far, 0)
     lax.fori_loop(1, half, send_near, 0)
     gather_block(me)
+    for load in loads[1:]:
+        load.wait()
 
     ones = jnp.ones((pk_ref.shape[0], HD), BF16)
     for g in range(kv_heads):
@@ -378,9 +405,15 @@
     return pl.pallas_call(
         functools.partial(kernel, n),
         out_shape=jax.ShapeDtypeStruct(queries.shape, BF16),
-        in_specs=[smem] * 3 + [vmem] * 5,
+        in_specs=[smem] * 3 + [pl.BlockSpec(memory_space=pltpu.HBM)] * 5,
         out_specs=vmem,
         scratch_shapes=[
+            pltpu.VMEM(queries.shape, BF16),
+            pltpu.VMEM(resp_keys.shape, BF16),
+            pltpu.VMEM(resp_values.shape, BF16),
+            pltpu.VMEM(prompt_keys.shape, BF16),
+            pltpu.VMEM(prompt_values.shape, BF16),
+            pltpu.SemaphoreType.DMA((5,)),
             pltpu.VMEM(block, BF16),
             pltpu.VMEM(slots, BF16),
             pltpu.VMEM(slots, BF16),
@@ -406,7 +439,7 @@
         ),
     )(
         shard_order,
-        response_prompt,
+        response_prompt.reshape(1, -1),
         response_lengths,
         queries,
         resp_keys,

time: 67.8 us -> 66.2 us (0.976)
  local copies, waits for them, and re-layouts: 3.19 us -> 1.88 us
    unnamed x2 -> x1, local copies, waits for them, and re-layouts: 3.19 us -> 1.88 us
where the time goes in v3:
time: 66.2 us; the launch traced here: 66 us
  Pallas kernels  64.1 us (97%)
  local copies, waits for them, and re-layouts  1.88 us (3%)
    pallas_call x1, Pallas kernels, per_device(): pl.pallas_call(functools.partial(kernel, n), out_shape=jax.ShapeDtypeStru...  64.1 us
    unnamed x1, local copies, waits for them, and re-layouts  1.88 us

profile of v3, /device:TPU:0, one launch (start us, length us, event | category | flops | bytes accessed | tf_op | source)
XLA Modules:
  0.0 66.0 jit_solution(5416347371952018381)
XLA Ops:
  0.0 64.1 %shard_map.82 = bf16[128,2048]{1,0:T(8,128)(2,1)} custom-call(s32[8]{0:T(128)} %order_ref.1, s32[1,4]{1,0:T(1,128)} %bitcast.1, s32[1,4]{1,0:T(1,128)} %len_ref.1, bf16[128,2048]{1,0:T(8,128)(2,1)} %q_hbm.1, bf16[128,256]{1,0:T(8,128)(2,1)} %rk_hbm.1, bf16[128,256]{1,0:T(8,128)(2,1)} %rv_hbm.1, bf16[1024,256]{1,0:T(8,128)(2,1)} %pk_hbm.1, ...), custom_call_target="tpu_custom_call" | custom-call | tf_op jit(solution)/shard_map/pallas_call | solution.py:405
  64.1 1.9 %copy.10 = bf16[128,2048]{1,0:T(8,128)(2,1)} copy(bf16[128,2048]{1,0:T(8,128)(2,1)} %shard_map.82) | data formatting | bytes 1048576
